TPU v7x, 256 devices: a whole 4x4x8 slice. The times are simulated.
256 devices in a mesh: lat: 32 (over z, x), lev: 8 (over y, core).
Axes of the slice: x: 4, y: 4, z: 8, core: 2. Of those that a mesh axis runs over, the one named last changes fastest.
Arguments:
- coeffs: bfloat16 [24, 2, 512, 1152], P(None, None, ('lat', 'lev')), may hold values from -12 to 12
- legendre: bfloat16 [512, 1152, 1280], P(('lat', 'lev')), may hold values from -0.1875 to 0.1875
- pair_first: int32 [512], replicated, may hold values from 0 to 511, each once
- row_counts: int32 [2560], replicated, may hold values from 20 to 5136, as said below
- quad_weights: float32 [1280], replicated, may hold values from 0.5 to 2
Outputs:
- flux_spectra: bfloat16 [16, 2, 512, 1152], P(None, None, ('lat', 'lev'))
Inputs may be any that keep to these rules, and one draw needn't show every extreme that they name: row_counts[i] is a multiple of 4 within 12 of 20 + 4 min(i, 2559 - i); the two polar rows hold 20 and the two rows beside the equator 5136.
All inputs are finite; a program needn't handle non-finite values.
Results may differ from a plain program's by a relative error of at most 0.0075.
Values may be sent and summed in bfloat16 or wider, within the bound.
A program may use at most 128 MiB of HBM per device.

v0:
```python
import math

import jax
import jax.numpy as jnp
from jax import lax
from jax.sharding import PartitionSpec as P

WAVES = 1024
NLON = 5136
LONPAD = 5248


def member_masks(leading, degrees, waves):
    entry = jnp.arange(degrees, dtype=jnp.int32)[None, :]
    border = (waves - leading)[:, None]
    member_one = (entry < border).astype(jnp.float32)
    member_two = ((entry >= border) & (entry <= waves)).astype(jnp.float32)
    sign_one = (1 - 2 * (entry % 2)).astype(jnp.float32) + 0.0 * member_one
    sign_two = (1 - 2 * ((entry + leading[:, None]) % 2)).astype(jnp.float32)
    return (member_one, member_two, sign_one, sign_two)


def wave_table(waves_col, n_lon, length):
    column = jnp.arange(length, dtype=jnp.int32)
    turns = waves_col[:, None] * column[None, :] % n_lon
    angle = turns.astype(jnp.float32) * (2.0 * math.pi / n_lon)
    scale = 1.0 / math.sqrt(n_lon)
    live = (column < n_lon)[None, :]
    cosine = jnp.where(live, jnp.cos(angle) * scale, 0.0)
    sine = jnp.where(live, -jnp.sin(angle) * scale, 0.0)
    return jnp.stack([cosine, sine]).astype(jnp.bfloat16)


def to_lat(values):
    return lax.all_to_all(values, "lat", split_axis=3, concat_axis=2, tiled=True)


def to_lev(values):
    return lax.all_to_all(values, "lev", split_axis=0, concat_axis=2, tiled=True)


def from_lev(values):
    return lax.all_to_all(values, "lev", split_axis=2, concat_axis=0, tiled=True)


def from_lat(values):
    return lax.all_to_all(values, "lat", split_axis=2, concat_axis=3, tiled=True)


def on_device(coeffs, legendre, pair_first, row_counts, quad_weights):
    rows_in, _, own_pairs, degrees = coeffs.shape
    half_lat = legendre.shape[2]
    all_lat = 2 * half_lat
    lat_count = lax.axis_size("lat")
    lev_count = lax.axis_size("lev")
    device = lax.axis_index("lat") * lev_count + lax.axis_index("lev")
    leading = lax.dynamic_slice_in_dim(pair_first, device * own_pairs, own_pairs)
    member_one, member_two, sign_one, sign_two = member_masks(leading, degrees, WAVES)
    selector = jnp.stack(
        [member_one, member_one * sign_one, member_two, member_two * sign_two]
    ).astype(jnp.bfloat16)
    spread = coeffs[None] * selector[:, None, None]
    products = jnp.einsum("qkrpt,ptl->qkrpl", spread, legendre, preferred_element_type=jnp.float32)
    north = jnp.stack([products[0], products[2]], axis=3)
    south = jnp.stack([products[1], products[3]], axis=3)
    fourier_rows = jnp.concatenate([north, south[..., ::-1]], axis=-1).astype(jnp.bfloat16)
    fourier_rows = fourier_rows.reshape(rows_in, 2, 2 * own_pairs, all_lat)
    swapped_first = (
        pair_first.reshape(lat_count, lev_count, own_pairs).transpose(1, 0, 2).reshape(-1)
    )
    arrived = to_lev(to_lat(fourier_rows))
    waves_col = jnp.stack([swapped_first, WAVES - 1 - swapped_first], axis=1).reshape(-1)
    lat_rows = arrived.shape[3]
    lat_start = lax.axis_index("lat") * lat_rows
    counts_here = lax.dynamic_slice_in_dim(row_counts, lat_start, lat_rows)
    wave_limit = jnp.minimum(WAVES - 1, counts_here // 2 - 1)
    keep_mask = (waves_col[:, None] <= wave_limit[None, :]).astype(jnp.float32)
    factor = jnp.where(waves_col == 0, 1.0, 2.0).astype(jnp.float32)[:, None]
    north_side = lat_start < half_lat
    mirror_start = jnp.where(north_side, lat_start, all_lat - lat_start - lat_rows)
    weight_slice = lax.dynamic_slice_in_dim(quad_weights, mirror_start, lat_rows)
    weight_here = jnp.where(north_side, weight_slice, weight_slice[::-1])
    table = wave_table(waves_col, NLON, LONPAD)
    scaled = arrived * (keep_mask * factor).astype(jnp.bfloat16)[None, None]
    grid_fields = jnp.einsum("krml,rmj->klj", scaled, table, preferred_element_type=jnp.float32)
    levels_here = grid_fields.shape[0] // 3
    fields = grid_fields.reshape(levels_here, 3, lat_rows, LONPAD)
    grid_flux = jnp.stack([fields[:, 0] * fields[:, 2], fields[:, 1] * fields[:, 2]], axis=1)
    grid_flux = grid_flux.reshape(2 * levels_here, lat_rows, LONPAD).astype(jnp.bfloat16)
    spectra = jnp.einsum("klj,rmj->krml", grid_flux, table, preferred_element_type=jnp.float32)
    weighted = (spectra * (keep_mask * weight_here[None, :])[None, None]).astype(jnp.bfloat16)
    returned = from_lat(from_lev(weighted))
    rows_out = returned.shape[0]
    returned = returned.reshape(rows_out, 2, own_pairs, 2, all_lat)
    north_part = returned[..., :half_lat]
    south_part = returned[..., half_lat:][..., ::-1]
    north_sum = jnp.einsum(
        "krpel,ptl->ekrpt", north_part, legendre, preferred_element_type=jnp.float32
    )
    south_sum = jnp.einsum(
        "krpel,ptl->ekrpt", south_part, legendre, preferred_element_type=jnp.float32
    )
    result = member_one * (north_sum[0] + sign_one * south_sum[0]) + member_two * (
        north_sum[1] + sign_two * south_sum[1]
    )
    return result.astype(jnp.bfloat16)


def solution(mesh):
    placed = (P(None, None, ("lat", "lev"), None), P(("lat", "lev"), None, None), P(), P(), P())
    return jax.shard_map(
        on_device,
        mesh=mesh,
        in_specs=placed,
        out_specs=P(None, None, ("lat", "lev"), None),
        check_vma=False,
    )
```

profile of v0, /device:TPU:1, one launch (start us, length us, event | category | flops | bytes accessed | tf_op | source)
XLA Modules:
  0.0 265.7 jit_solution(16185784635383659440)
XLA Ops:
  1.1 1.0 copy.68
  2.1 4.1 %fusion.18 = bf16[4,24,2,2,1280]{4,1,2,0,3:T(8,128)(2,1)S(1)} fusion(bf16[2,1152,1280]{2,1,0:T(8,128)(2,1)} %param.6, bf16[4,2,1152]{2,0,1:T(4,128)(2,1)S(1)} %pad_maximum_fusion.6, bf16[24,2,2,1152]{3,0,1,2:T(8,128)(2,1)S(1)} %copy.68), kind=kOutput, calls=%fused_computation.21 | convolution fusion | flops 1132904448 | bytes 7120896 | tf_op jit(solution)/shard_map/qkrpt,ptl->qkrpl/dot_general | solution.py:63
  6.4 1.1 rev.9
  7.7 5.2 %copy.73 = bf16[24,2,4,2560]{0,2,1,3:T(4,128)(2,1)} copy(bf16[24,2,4,2560]{3,0,2,1:T(8,128)(2,1)S(1)} %pad_maximum_fusion.4) | data formatting | bytes 1966080 | tf_op jit(solution)/shard_map/concatenate | solution.py:66
  12.9 13.8 %reshape.712 = bf16[32,2,7680]{2,1,0:T(2,128)(2,1)} reshape(bf16[2560,2,4,24]{3,2,1,0:T(4,128)(2,1)} %bitcast.122) | data formatting | bytes 1966080
  26.7 12.0 %all-to-all-start = ((bf16[32,2,7680]{2,1,0:T(2,128)(2,1)}), bf16[32,2,7680]{2,1,0:T(2,128)(2,1)S(1)}, u32[]{:S(2)}, u32[]{:S(2)}) async-start(bf16[32,2,7680]{2,1,0:T(2,128)(2,1)} %reshape.712), calls=%async_computation | async-start | bytes 1966080 | tf_op jit(solution)/shard_map/all_to_all | solution.py:35
  41.1 93.0 %select_convert_fusion.1 = (bf16[1,1024,5248]{2,1,0:T(8,128)(2,1)}, bf16[1,1024,5248]{2,1,0:T(8,128)(2,1)}) fusion(s32[1024]{0:T(1024)S(1)} %mul.205, pred[5248]{0:T(1024)(128)(4,1)S(1)} %iota_compare_fusion), kind=kLoop, calls=%fused_computation.9 | loop fusion | flops 85983232 | bytes 21505152 | tf_op jit(solution)/shard_map/convert.16
  134.1 8.6 %reshape.713 = bf16[2560,2,4,24]{3,2,1,0:T(4,128)(2,1)} reshape(bf16[32,2,7680]{2,1,0:T(2,128)(2,1)S(1)} %all-to-all-done) | data formatting | bytes 1966080
  142.7 5.8 %copy.74 = bf16[24,2,4,32,80]{4,0,2,3,1:T(8,128)(2,1)S(1)} copy(bf16[24,2,4,32,80]{0,2,1,4,3:T(4,128)(2,1)} %bitcast.123) | data formatting | bytes 1966080 | tf_op jit(solution)/shard_map/all_to_all | solution.py:35
  148.5 1.8 copy.75
  150.3 5.6 %all-to-all-start.1 = ((bf16[24,2,128,80]{2,3,1,0:T(8,128)(2,1)}), bf16[24,2,128,80]{2,3,1,0:T(8,128)(2,1)S(1)}, u32[]{:S(2)}, u32[]{:S(2)}) async-start(bf16[24,2,128,80]{2,3,1,0:T(8,128)(2,1)} %copy.75), calls=%async_computation.1 | async-start | bytes 1966080 | tf_op jit(solution)/shard_map/all_to_all | solution.py:39
  157.5 12.7 %all-to-all-done.1 = bf16[24,2,128,80]{2,3,1,0:T(8,128)(2,1)S(1)} async-done(((bf16[24,2,128,80]{2,3,1,0:T(8,128)(2,1)}), bf16[24,2,128,80]{2,3,1,0:T(8,128)(2,1)S(1)}, u32[]{:S(2)}, u32[]{:S(2)}) %all-to-all-start.1) | async-done | bytes 983072 | tf_op jit(solution)/shard_map/all_to_all | solution.py:39
  170.2 11.9 %fusion.9 = f32[1,3,80,5248]{3,2,1,0:T(8,128)} fusion(bf16[1,1024,5248]{2,1,0:T(8,128)(2,1)} %get-tuple-element.16, bf16[1,1024,5248]{2,1,0:T(8,128)(2,1)} %get-tuple-element.15, bf16[8,3,2,10,8,128]{5,4,3,2,1,0:T(8,128)(2,1)S(1)} %bitcast.132, bf16[1024,80]{0,1:T(8,128)(2,1)S(1)} %fusion.41), kind=kOutput, calls=%fused_computation.14 | convolution fusion | flops 5170233344 | bytes 27680768 | tf_op jit(solution)/shard_map/krml,rmj->klj/dot_general | solution.py:85
  182.2 2.7 %fusion.28 = (bf16[1,1,80,5248]{3,2,1,0:T(8,128)(2,1)S(1)}, bf16[1,1,80,5248]{3,2,1,0:T(8,128)(2,1)S(1)}) fusion(f32[1,3,80,5248]{3,2,1,0:T(8,128)} %fusion.9), kind=kLoop, calls=%fused_computation.27 | loop fusion | flops 1679360 | bytes 6717440 | tf_op jit(solution)/shard_map/convert
  184.9 9.8 %fusion.34 = bf16[2,2,1024,80]{2,3,0,1:T(8,128)(2,1)S(1)} fusion(bf16[1,1,80,5248]{3,2,1,0:T(8,128)(2,1)S(1)} %get-tuple-element.8, bf16[1,1,80,5248]{3,2,1,0:T(8,128)(2,1)S(1)} %get-tuple-element.7, bf16[1,1024,5248]{2,1,0:T(8,128)(2,1)} %get-tuple-element.16, bf16[1,1024,5248]{2,1,0:T(8,128)(2,1)S(1)} %bitcast.125, f32[1024,80]{0,1:T(8,128)S(1)} %copy-done), kind=kOutput, calls=%fused_computation.36 | convolution fusion | flops 3486334976 | bytes 24158208 | tf_op jit(solution)/shard_map/klj,rmj->krml/dot_general | solution.py:90
  194.8 0.8 copy.77
  195.6 18.3 %all_to_all.69 = bf16[2,2,1024,80]{3,0,1,2:T(2,128)(2,1)S(1)} all-to-all(bf16[2,2,1024,80]{3,0,1,2:T(2,128)(2,1)S(1)} %copy.77), channel_id=1, replica_groups=mesh['lat'=32,'lev'=8] {'lev'}, dimensions={2} | all-to-all | bytes 1310720 | tf_op jit(solution)/shard_map/all_to_all | solution.py:43
  214.6 2.0 copy.80
  216.7 9.3 %all-to-all-start.3 = ((bf16[16,2,128,80]{3,1,0,2:T(2,128)(2,1)}), bf16[16,2,128,80]{3,1,0,2:T(2,128)(2,1)S(1)}, u32[]{:S(2)}, u32[]{:S(2)}) async-start(bf16[16,2,128,80]{3,1,0,2:T(2,128)(2,1)} %copy.80), calls=%async_computation.3 | async-start | bytes 2097152 | tf_op jit(solution)/shard_map/all_to_all | solution.py:47
  226.2 25.7 %all-to-all-done.3 = bf16[16,2,128,80]{3,1,0,2:T(2,128)(2,1)S(1)} async-done(((bf16[16,2,128,80]{3,1,0,2:T(2,128)(2,1)}), bf16[16,2,128,80]{3,1,0,2:T(2,128)(2,1)S(1)}, u32[]{:S(2)}, u32[]{:S(2)}) %all-to-all-start.3) | async-done | bytes 655392 | tf_op jit(solution)/shard_map/all_to_all | solution.py:47
  252.7 2.1 reshape.707
  254.8 1.0 rev.11
  255.8 4.5 %fusion.24 = f32[2,16,2,2,1152]{4,1,2,3,0:T(8,128)S(1)} fusion(bf16[2,1152,1280]{2,1,0:T(8,128)(2,1)} %param.6, bf16[16,2,2,2,1280]{4,0,3,2,1:T(8,128)(2,1)S(1)} %rev.11), kind=kOutput, calls=%fused_computation.23 | convolution fusion | flops 377487360 | bytes 6815744 | tf_op jit(solution)/shard_map/krpel,ptl->ekrpt/dot_general | solution.py:100
  260.3 4.5 %fusion.21 = f32[2,16,2,2,1152]{4,1,0,2,3:T(8,128)S(1)} fusion(bf16[2,1152,1280]{2,1,0:T(8,128)(2,1)} %param.6, bf16[16,2,2,2,1280]{4,0,3,2,1:T(8,128)(2,1)S(1)} %get-tuple-element.13), kind=kOutput, calls=%fused_computation.22 | convolution fusion | flops 377487360 | bytes 6815744 | tf_op jit(solution)/shard_map/krpel,ptl->ekrpt/dot_general | solution.py:97
  (47 shorter events, 8.0 us)
Async XLA Ops:
  6.3 32.5 %copy-start.1 = (s32[512]{0:T(512)S(1)}, s32[512]{0:T(512)}, u32[]{:S(2)}) copy-start(s32[512]{0:T(512)} %param.7) | copy-start | bytes 6148
  26.7 107.4 %all-to-all-start = ((bf16[32,2,7680]{2,1,0:T(2,128)(2,1)}), bf16[32,2,7680]{2,1,0:T(2,128)(2,1)S(1)}, u32[]{:S(2)}, u32[]{:S(2)}) async-start(bf16[32,2,7680]{2,1,0:T(2,128)(2,1)} %reshape.712), calls=%async_computation | async-start | bytes 1966080 | tf_op jit(solution)/shard_map/all_to_all | solution.py:35
  150.3 34.6 %slice-start = ((s8[10747904]{0:T(1024)(128)(4,1)}), s8[2359296]{0:T(1024)(128)(4,1)S(1)}, s32[]{:S(2)}) async-start(s8[10747904]{0:T(1024)(128)(4,1)} %bitcast.124), calls=%async_computation.4 | async-start | bytes 4718592
  150.3 20.0 %all-to-all-start.1 = ((bf16[24,2,128,80]{2,3,1,0:T(8,128)(2,1)}), bf16[24,2,128,80]{2,3,1,0:T(8,128)(2,1)S(1)}, u32[]{:S(2)}, u32[]{:S(2)}) async-start(bf16[24,2,128,80]{2,3,1,0:T(8,128)(2,1)} %copy.75), calls=%async_computation.1 | async-start | bytes 1966080 | tf_op jit(solution)/shard_map/all_to_all | solution.py:39
  170.2 14.7 %slice-start.1 = ((s8[10747904]{0:T(1024)(128)(4,1)}), s8[4194304]{0:T(1024)(128)(4,1)S(1)}, s32[]{:S(2)}) async-start(s8[10747904]{0:T(1024)(128)(4,1)} %bitcast.124), calls=%async_computation.5 | async-start | bytes 8388608
  170.2 14.7 %slice-start.2 = ((s8[10747904]{0:T(1024)(128)(4,1)}), s8[4194304]{0:T(1024)(128)(4,1)S(1)}, s32[]{:S(2)}) async-start(s8[10747904]{0:T(1024)(128)(4,1)} %bitcast.124), calls=%async_computation.6 | async-start | bytes 8388608
  170.2 14.7 %copy-start = (f32[1024,80]{0,1:T(8,128)S(1)}, f32[1024,80]{0,1:T(8,128)}, u32[]{:S(2)}) copy-start(f32[1024,80]{0,1:T(8,128)} %compare_select_fusion) | copy-start | bytes 983044
  216.7 35.2 %all-to-all-start.3 = ((bf16[16,2,128,80]{3,1,0,2:T(2,128)(2,1)}), bf16[16,2,128,80]{3,1,0,2:T(2,128)(2,1)S(1)}, u32[]{:S(2)}, u32[]{:S(2)}) async-start(bf16[16,2,128,80]{3,1,0,2:T(2,128)(2,1)} %copy.80), calls=%async_computation.3 | async-start | bytes 2097152 | tf_op jit(solution)/shard_map/all_to_all | solution.py:47
where the time goes:
time: 268 us; the launch traced here: 266 us
  other arithmetic  99.7 us (37%)
  local copies, waits for them, and re-layouts  47.1 us (18%)
  waiting for transfers between devices  38.4 us (14%)
  matrix products  34.9 us (13%)
  starting transfers between devices  26.9 us (10%)
  blocking collectives  18.3 us (7%)
    another operation x5, other arithmetic  96 us
    all_to_all x1, waiting for transfers between devices, from_lat(): lax.all_to_all(values, 'lat', split_axis=2, concat_axis=3, tiled=True)  25.7 us
    unnamed x13, local copies, waits for them, and re-layouts  23.4 us
    all_to_all x1, blocking collectives, from_lev(): lax.all_to_all(values, 'lev', split_axis=2, concat_axis=0, tiled=True)  18.3 us
    all_to_all x1, waiting for transfers between devices, to_lev(): lax.all_to_all(values, 'lev', split_axis=0, concat_axis=2, tiled=True)  12.7 us
    all_to_all x1, starting transfers between devices, to_lat(): lax.all_to_all(values, 'lat', split_axis=3, concat_axis=2, tiled=True)  12 us
    dot_general x1, matrix products, on_device(): jnp.einsum('krml,rmj->klj', scaled, table, preferred_element_type=jnp.flo...  11.9 us
    dot_general x1, matrix products, on_device(): jnp.einsum('klj,rmj->krml', grid_flux, table, preferred_element_type=jnp....  9.84 us
  transfers between devices with their start and end apart: 3, of which 2 were waited for; matrix products, arithmetic and copies ran while one was open for 37% of the time, Pallas kernels for 0%

commit v1 on v0

v1 whole, which is shorter than its diff:
```python
import functools

import jax
import jax.numpy as jnp
import ml_dtypes
import numpy as np
from jax import lax
from jax.experimental import pallas as pl
from jax.experimental.pallas import tpu as pltpu
from jax.sharding import PartitionSpec as P

MESH = pl.DeviceIdType.MESH
F32 = jnp.float32
BF16 = jnp.bfloat16
WAVES = 1024
NLON = 5136
QUARTER = NLON // 4
JPAD = 1408
HALF = WAVES // 2
PAIRLEN = 1152
HLAT = 1280
LATS = 32
LEVS = 8
RLEN = HLAT // LATS
LANES = 128
LTILES = HLAT // LANES
KIN = 24
DEVICES = LATS * LEVS
JTILES = ((0, 256), (256, 256), (512, 256), (768, 256), (1024, 256), (1280, 128))


def table_constant():
    column = np.arange(JPAD, dtype=np.int64)[None, :]
    row = np.arange(HALF, dtype=np.int64)[:, None]
    live = column <= QUARTER
    scale = 1.0 / np.sqrt(NLON)
    parts = []
    for fn in (np.cos, lambda x: -np.sin(x)):
        for wave in (2 * row, WAVES - 1 - 2 * row):
            angle = (wave * column % NLON) * (2.0 * np.pi / NLON)
            parts.append(np.where(live, fn(angle) * scale, 0.0))
    return np.concatenate(parts, axis=1).astype(np.float32).astype(ml_dtypes.bfloat16)


def coords():
    a, b = lax.axis_index("lat"), lax.axis_index("lev")
    return a // 4, a % 4, b // 2, b % 2


def lat_peer(i):
    z, x, _, _ = coords()
    return ((z + i % 8) % 8) * 4 + (x + i // 8) % 4


def lev_peer(i):
    _, _, y, c = coords()
    return ((y + i // 2) % 4) * 2 + (c + i % 2) % 2


def lane_iota(rows):
    return lax.broadcasted_iota(jnp.int32, (rows, LANES), 1)


def left(x, by):
    by = by % LANES
    return x if by == 0 else pltpu.roll(x, LANES - by, 1)


def kernel(
    coeffs, leg_hbm, tab_hbm, first_smem, first_row, limits, quad, out,
    leg, tab0, tab, ys, send, recv, xs, xt, flux, send_back, recv_back, dsp, rs, mw,
    leg_sem, tab_sem, own_sem, send_sem, recv_sem, back_send_sem, back_recv_sem, ready_sem,
):
    a_me, b_me = lax.axis_index("lat"), lax.axis_index("lev")
    me = a_me * LEVS + b_me

    barrier = pltpu.get_barrier_semaphore()

    def greet_lev(i, carry):
        pl.semaphore_signal(barrier, inc=1, device_id=(a_me, lev_peer(i)), device_id_type=MESH)
        return carry

    def greet_lat(i, carry):
        pl.semaphore_signal(barrier, inc=1, device_id=(lat_peer(i), b_me), device_id_type=MESH)
        return carry

    leg_copies = [pltpu.make_async_copy(leg_hbm.at[p], leg.at[p], leg_sem.at[p]) for p in range(2)]
    tab_copy = pltpu.make_async_copy(tab_hbm, tab0, tab_sem)
    for copy in leg_copies:
        copy.start()
    tab_copy.start()
    lax.fori_loop(1, LEVS, greet_lev, 0)
    lax.fori_loop(1, LATS, greet_lat, 0)

    entry = lax.broadcasted_iota(jnp.int32, (1, PAIRLEN), 1)
    alternating = (1 - 2 * (entry % 2)).astype(F32)
    masks, signs = [], []
    for p in range(2):
        first = first_smem[2 * me + p]
        border = WAVES - first
        is_odd = first % 2
        one = (entry < border).astype(F32)
        two = ((entry >= border) & (entry <= WAVES)).astype(F32)
        odd = is_odd.astype(F32)
        masks.append((one + odd * (two - one), two + odd * (one - two)))
        signs.append((alternating * (1.0 - 2.0 * odd), alternating))
        even_wave = first + is_odd * (WAVES - 1 - 2 * first)
        waves = (even_wave, WAVES - 1 - even_wave)
        factors = [jnp.where(w == 0, 1.0, 2.0) for w in waves]
        kept = [[(limits[s : s + 1, :] >= w).astype(F32) for w in waves] for s in range(2)]
        rows = []
        for side in range(2):
            for c in range(2):
                values = coeffs[p, c].astype(F32)
                for par in range(2):
                    chosen = masks[p][par] * signs[p][par] if side else masks[p][par]
                    rows.append(values * chosen)
                    mw[p * 8 + side * 4 + c * 2 + par : p * 8 + side * 4 + c * 2 + par + 1, :] = (
                        kept[side][par] * quad[...]
                    )
        spread = jnp.concatenate(rows, axis=0).astype(BF16)
        leg_copies[p].wait()
        for lt in range(0, LTILES, 2):
            at = lt * LANES
            product = jnp.dot(spread, leg[p, :, at : at + 2 * LANES], preferred_element_type=F32)
            for side in range(2):
                for par in range(2):
                    scale = kept[side][par][:, at : at + 2 * LANES] * factors[par]
                    for c in range(2):
                        kind = side * 4 + c * 2 + par
                        piece = product[kind * KIN : (kind + 1) * KIN] * scale
                        for half in range(2):
                            ys[lt + half, p * 192 + kind * KIN : p * 192 + (kind + 1) * KIN, :] = piece[
                                :, half * LANES : (half + 1) * LANES
                            ]

    pl.semaphore_wait(barrier, LEVS - 1 + LATS - 1)

    def greet_ready(i, carry):
        pl.semaphore_signal(ready_sem, inc=1, device_id=(lat_peer(i), b_me), device_id_type=MESH)
        return carry

    lax.fori_loop(1, LATS, greet_ready, 0)

    lane16 = lane_iota(16)

    def make_and_send(i, carry):
        b = lev_peer(i)
        fields = [
            [ys[lt, pl.ds(3 * b + f, 16, stride=KIN), :] for lt in range(LTILES)] for f in range(3)
        ]
        for a in range(LATS):
            tile, shift = divmod(a * RLEN, LANES)
            parts = []
            for f in range(3):
                part = fields[f][tile]
                if shift + RLEN > LANES:
                    part = jnp.where(lane16 >= shift, part, fields[f][tile + 1])
                parts.append(left(part, shift - f * RLEN))
            block = jnp.where(lane16 < RLEN, parts[0], jnp.where(lane16 < 2 * RLEN, parts[1], parts[2]))
            send[a, b] = block.astype(BF16)

        @pl.when(i == 0)
        def _():
            pl.semaphore_wait(ready_sem, LATS - 1)

        def go(l, carry):
            a = lat_peer(l)
            pltpu.make_async_remote_copy(
                src_ref=send.at[a, b],
                dst_ref=recv.at[me],
                send_sem=send_sem,
                recv_sem=recv_sem,
                device_id=(a, b),
                device_id_type=MESH,
            ).start()
            return carry

        lax.fori_loop(jnp.where(i == 0, 1, 0), LATS, go, 0)
        return carry

    lax.fori_loop(0, LEVS, make_and_send, 0)
    own = pltpu.make_async_copy(send.at[a_me, b_me], recv.at[me], own_sem)
    own.start()

    tab_copy.wait()
    firsts = first_row[...]
    slot_row = jnp.where(firsts % 2 == 0, firsts, WAVES - 1 - firsts) // 2
    chosen = (lax.broadcasted_iota(jnp.int32, (HALF, HALF), 0) == slot_row).astype(F32)
    pick = jnp.transpose(chosen).astype(BF16)

    def permute(n, carry):
        at = pl.ds(pl.multiple_of(n * 256, 256), 256)
        tab[:, at] = jnp.dot(pick, tab0[:, at], preferred_element_type=F32).astype(BF16)
        return carry

    lax.fori_loop(0, 4 * JPAD // 256, permute, 0)

    own.wait()
    others = pl.ds(0, DEVICES - 1)
    pltpu.make_async_copy(recv.at[others], recv.at[others], recv_sem).wait()

    def unpack(n, carry):
        blocks = recv[pl.ds(n * 16, 16)].astype(F32).reshape(256, LANES)
        xs[pl.ds(pl.multiple_of(n * 256, 256), 256), :] = blocks
        return carry

    lax.fori_loop(0, DEVICES // 16, unpack, 0)
    for side in range(2):
        for cp in range(4):
            for q in range(4):
                block = xs[pl.ds(q * 1024 + side * 4 + cp, LANES, stride=8), :]
                xt[cp, side * LANES : (side + 1) * LANES, q * LANES : (q + 1) * LANES] = jnp.transpose(
                    block
                ).astype(BF16)

    for cp in range(4):
        for side in range(2):
            flux[cp, side * LANES + 2 * RLEN : (side + 1) * LANES, :] = jnp.zeros((LANES - 2 * RLEN, JPAD), BF16)
    for at, width in JTILES:
        ce, co, se, so = (
            jnp.dot(xt[cp], tab[:, cp * JPAD + at : cp * JPAD + at + width], preferred_element_type=F32)
            for cp in range(4)
        )
        column = at + lax.broadcasted_iota(jnp.int32, (1, width), 1)
        half = jnp.where((column == 0) | (column == QUARTER), 0.5, 1.0)
        plus, minus, sums, diffs = ce + co, ce - co, se + so, se - so
        grids = (plus + sums, plus - sums, minus - diffs, minus + diffs)
        for side in range(2):
            base = side * LANES
            fl = []
            for g in grids:
                q = g[base + 2 * RLEN : base + 3 * RLEN] * half
                fl.append(g[base : base + 2 * RLEN] * jnp.concatenate([q, q], axis=0))
            s12, d12, s34, d34 = fl[0] + fl[1], fl[0] - fl[1], fl[2] + fl[3], fl[3] - fl[2]
            for cp, value in enumerate((s12 + s34, s12 - s34, d12 + d34, d12 - d34)):
                flux[cp, base : base + 2 * RLEN, at : at + width] = value.astype(BF16)

    for cp in range(4):
        spectra = lax.dot_general(
            tab[:, cp * JPAD : (cp + 1) * JPAD], flux[cp], (((1,), (1,)), ((), ())), preferred_element_type=F32
        )
        for side in range(2):
            xs[pl.ds(side * 4 + cp, HALF, stride=8), :] = spectra[:, side * LANES : (side + 1) * LANES]

    def pack(n, carry):
        rows = xs[pl.ds(pl.multiple_of(n * 256, 256), 256), :]
        send_back[pl.ds(n * 16, 16)] = rows.reshape(16, 16, LANES).astype(BF16)
        return carry

    lax.fori_loop(0, DEVICES // 16, pack, 0)

    def go_back(i, carry):
        a, b = lat_peer(i % LATS), lev_peer(i // LATS)
        pltpu.make_async_remote_copy(
            src_ref=send_back.at[a * LEVS + b],
            dst_ref=recv_back.at[me],
            send_sem=back_send_sem,
            recv_sem=back_recv_sem,
            device_id=(a, b),
            device_id_type=MESH,
        ).start()
        return carry

    lax.fori_loop(1, DEVICES, go_back, 0)
    own = pltpu.make_async_copy(send_back.at[me], recv_back.at[me], own_sem)
    own.start()
    own.wait()
    pltpu.make_async_copy(recv_back.at[others], recv_back.at[others], back_recv_sem).wait()

    def gather(b, carry):
        blocks = [recv_back[a * LEVS + b].astype(F32) for a in range(LATS)]
        for lt in range(LTILES):
            comps = []
            for comp in range(2):
                whole = None
                for a in range(lt * LANES // RLEN, (lt * LANES + LANES - 1) // RLEN + 1):
                    start = a * RLEN - lt * LANES
                    part = left(blocks[a], comp * RLEN - start)
                    whole = part if whole is None else jnp.where(lane16 >= start, part, whole)
                comps.append(whole * mw[:, lt * LANES : (lt + 1) * LANES])
            for p in range(2):
                both = jnp.concatenate([comps[0][p * 8 : p * 8 + 8], comps[1][p * 8 : p * 8 + 8]], axis=0)
                dsp[p, pl.ds(pl.multiple_of(b * 16, 16), 16), lt * LANES : (lt + 1) * LANES] = both.astype(BF16)
        return carry

    lax.fori_loop(0, LEVS, gather, 0)

    for p in range(2):
        for n in range(PAIRLEN // LANES):
            rs[n] = lax.dot_general(
                dsp[p], leg[p, n * LANES : (n + 1) * LANES, :], (((1,), (1,)), ((), ())), preferred_element_type=F32
            )
            at = slice(n * LANES, (n + 1) * LANES)
            for c in range(2):
                total = None
                for par in range(2):
                    north = rs[n, pl.ds(c * 2 + par, 16, stride=8), :]
                    south = rs[n, pl.ds(4 + c * 2 + par, 16, stride=8), :]
                    term = masks[p][par][:, at] * (north + signs[p][par][:, at] * south)
                    total = term if total is None else total + term
                out[p, c, :, at] = total.astype(BF16)

    pltpu.make_async_copy(recv.at[others], recv.at[others], send_sem).wait()
    pltpu.make_async_copy(recv_back.at[others], recv_back.at[others], back_send_sem).wait()


def on_device(table, coeffs, legendre, pair_first, row_counts, quad_weights):
    swapped = coeffs.transpose(2, 1, 0, 3)
    counts = jnp.stack([row_counts[:HLAT], row_counts[HLAT:][::-1]])
    limits = jnp.minimum(WAVES - 1, counts // 2 - 1)
    vmem = pl.BlockSpec(memory_space=pltpu.VMEM)
    any_space = pl.BlockSpec(memory_space=pl.ANY)
    result = pl.pallas_call(
        kernel,
        out_shape=jax.ShapeDtypeStruct((2, 2, 16, PAIRLEN), BF16),
        in_specs=[vmem, any_space, any_space, pl.BlockSpec(memory_space=pltpu.SMEM), vmem, vmem, vmem],
        out_specs=vmem,
        scratch_shapes=[
            pltpu.VMEM((2, PAIRLEN, HLAT), BF16),
            pltpu.VMEM((HALF, 4 * JPAD), BF16),
            pltpu.VMEM((HALF, 4 * JPAD), BF16),
            pltpu.VMEM((LTILES, 384, LANES), F32),
            pltpu.VMEM((LATS, LEVS, 16, LANES), BF16),
            pltpu.VMEM((DEVICES, 16, LANES), BF16),
            pltpu.VMEM((DEVICES * 16, LANES), F32),
            pltpu.VMEM((4, 256, HALF), BF16),
            pltpu.VMEM((4, 256, JPAD), BF16),
            pltpu.VMEM((DEVICES, 16, LANES), BF16),
            pltpu.VMEM((DEVICES, 16, LANES), BF16),
            pltpu.VMEM((2, 128, HLAT), BF16),
            pltpu.VMEM((PAIRLEN // LANES, 128, LANES), F32),
            pltpu.VMEM((16, HLAT), F32),
            pltpu.SemaphoreType.DMA((2,)),
            pltpu.SemaphoreType.DMA,
            pltpu.SemaphoreType.DMA,
            pltpu.SemaphoreType.DMA,
            pltpu.SemaphoreType.DMA,
            pltpu.SemaphoreType.DMA,
            pltpu.SemaphoreType.DMA,
            pltpu.SemaphoreType.REGULAR,
        ],
        compiler_params=pltpu.CompilerParams(
            collective_id=0, has_side_effects=True, vmem_limit_bytes=52 * 2**20
        ),
        name="transforms",
    )(swapped, legendre, table, pair_first, pair_first.reshape(1, HALF), limits, quad_weights.reshape(1, HLAT))
    return result.transpose(2, 1, 0, 3)


def solution(mesh):
    placed = (P(None, None, ("lat", "lev"), None), P(("lat", "lev"), None, None), P(), P(), P())
    table = table_constant()
    return jax.shard_map(
        functools.partial(on_device, table),
        mesh=mesh,
        in_specs=placed,
        out_specs=P(None, None, ("lat", "lev"), None),
        check_vma=False,
    )
```

time: 268 us -> 80 us (0.30)
  other arithmetic: 99.7 us -> 0.04 us
  Pallas kernels: 0 us -> 75.7 us
  local copies, waits for them, and re-layouts: 47.1 us -> 3.99 us
  waiting for transfers between devices: 38.4 us -> 0 us
  matrix products: 34.9 us -> 0 us
  starting transfers between devices: 26.9 us -> 0 us
  blocking collectives: 18.3 us -> 0 us
    another operation x8 -> x0, other arithmetic: 96.1 us -> none
    pallas_call x0 -> x1, Pallas kernels: none -> 75.7 us  [on_device(): pl.pallas_call(kernel, out_shape=jax.ShapeDtypeStruct((2, 2, 16, PAIRLEN)...]
    all_to_all x3 -> x0, waiting for transfers between devices: 38.4 us -> none  [the longest x1 25.7 us: from_lat(): lax.all_to_all(values, 'lat', split_axis=2, concat_axis=3, tiled=True)]
    dot_general x5 -> x0, matrix products: 34.9 us -> none  [the longest x1 11.9 us: on_device(): jnp.einsum('krml,rmj->klj', scaled, table, preferred_element_type=jnp.flo...]
    all_to_all x3 -> x0, starting transfers between devices: 26.9 us -> none  [the longest x1 12 us: to_lat(): lax.all_to_all(values, 'lat', split_axis=3, concat_axis=2, tiled=True)]
    unnamed x13 -> x3, local copies, waits for them, and re-layouts: 23.4 us -> 1.64 us
    all_to_all x1 -> x0, blocking collectives: 18.3 us -> none  [from_lev(): lax.all_to_all(values, 'lev', split_axis=2, concat_axis=0, tiled=True)]
    all_to_all x6 -> x0, local copies, waits for them, and re-layouts: 11.1 us -> none  [the longest x2 7.57 us: to_lat(): lax.all_to_all(values, 'lat', split_axis=3, concat_axis=2, tiled=True)]
  transfers between devices with their start and end apart: 3 -> 0, of which waited for: 2 -> 0; matrix products, arithmetic and copies ran while one was open for 37% -> 0% of each run, Pallas kernels for 0% -> 0%
where the time goes in v1:
time: 80 us; the launch traced here: 79.8 us
  Pallas kernels  75.7 us (95%)
  local copies, waits for them, and re-layouts  3.99 us (5%)
    pallas_call x1, Pallas kernels, on_device(): pl.pallas_call(kernel, out_shape=jax.ShapeDtypeStruct((2, 2, 16, PAIRLEN)...  75.7 us
    unnamed x3, local copies, waits for them, and re-layouts  1.64 us

profile of v1, /device:TPU:1, one launch (start us, length us, event | category | flops | bytes accessed | tf_op | source)
XLA Modules:
  0.0 79.8 jit_solution(8159580624637440910)
XLA Ops:
  0.0 0.7 reshape.7.quad
  0.7 0.8 fusion
  1.5 0.1 rev.3
  1.6 1.0 %copy.10 = bf16[24,2,2,1152]{3,0,1,2:T(8,128)(2,1)S(1)} copy(bf16[24,2,2,1152]{3,2,1,0:T(2,128)(2,1)} %param.6) | data formatting | bytes 442368 | tf_op args[0]
  2.6 0.0 copy-start
  2.6 0.7 copy-done
  3.3 75.7 %transforms.1 = bf16[2,2,16,1152]{3,2,1,0:T(8,128)(2,1)S(1)} custom-call(bf16[2,2,24,1152]{3,2,1,0:T(8,128)(2,1)S(1)} %bitcast.5, bf16[2,1152,1280]{2,1,0:T(8,128)(2,1)} %leg_hbm.1, bf16[512,5632]{1,0:T(8,128)(2,1)} %constant.20.clone.tab_hbm, s32[512]{0:T(512)S(1)} %copy-done, s32[1,512]{1,0:T(1,128)S(1)} %bitcast.7, s32[2,1280]{1,0:T(2,128)S(1)} %add_minimum_fusion.limits, ...), custom_call_target="tpu_custom_call" | custom-call | tf_op jit(solution)/shard_map/transforms/pallas_call | solution.py:314
  79.0 0.8 copy.8
  (3 shorter events, 0.1 us)
Async XLA Ops:
  2.6 0.7 copy-start

commit v2 on v1

v2 whole, which is shorter than its diff:
```python
import functools

import jax
import jax.numpy as jnp
import ml_dtypes
import numpy as np
from jax import lax
from jax.experimental import pallas as pl
from jax.experimental.pallas import tpu as pltpu
from jax.sharding import PartitionSpec as P

MESH = pl.DeviceIdType.MESH
F32 = jnp.float32
BF16 = jnp.bfloat16
WAVES = 1024
NLON = 5136
QUARTER = NLON // 4
JPAD = 1408
HALF = WAVES // 2
PAIRLEN = 1152
HLAT = 1280
LATS = 32
LEVS = 8
RLEN = HLAT // LATS
LANES = 128
LTILES = HLAT // LANES
KIN = 24
DEVICES = LATS * LEVS
JTILES = ((0, 256), (256, 256), (512, 256), (768, 256), (1024, 256), (1280, 128))


def table_constant():
    column = np.arange(JPAD, dtype=np.int64)[None, :]
    row = np.arange(HALF, dtype=np.int64)[:, None]
    live = column <= QUARTER
    scale = 1.0 / np.sqrt(NLON)
    parts = []
    for fn in (np.cos, lambda x: -np.sin(x)):
        for wave in (2 * row, WAVES - 1 - 2 * row):
            angle = (wave * column % NLON) * (2.0 * np.pi / NLON)
            parts.append(np.where(live, fn(angle) * scale, 0.0))
    return np.concatenate(parts, axis=1).astype(np.float32).astype(ml_dtypes.bfloat16)


def coords():
    a, b = lax.axis_index("lat"), lax.axis_index("lev")
    return a >> 2, a & 3, b >> 1, b & 1


def device(z, x, y, c):
    return ((z & 7) << 2) + (x & 3), ((y & 3) << 1) + (c & 1)


def signal(sem, to):
    pl.semaphore_signal(sem, inc=1, device_id=to, device_id_type=MESH)


def lane_iota(rows):
    return lax.broadcasted_iota(jnp.int32, (rows, LANES), 1)


def left(x, by):
    by = by % LANES
    return x if by == 0 else pltpu.roll(x, LANES - by, 1)


def kernel(
    coeffs_hbm, leg_hbm, tab_hbm, first_hbm, counts_hbm, weights_hbm, out,
    coeffs, first_row, counts, weights, leg, tab0, tab, ys, send, recv, xs, xt, flux, send_lev, mid, send_lat, last, dt, dsp, rs, mw,
    leg_sem, tab_sem, own_sem, send_sem, recv_sem, lev_send_sem, lev_recv_sem, lat_send_sem, lat_recv_sem,
    round_sem, small_sem,
):
    a_me, b_me = lax.axis_index("lat"), lax.axis_index("lev")
    me = a_me * LEVS + b_me
    z_me, x_me, y_me, c_me = coords()

    half_lanes = HLAT // 2
    leg_copies = [
        [
            pltpu.make_async_copy(
                leg_hbm.at[p, :, pl.ds(h * half_lanes, half_lanes)],
                leg.at[p, :, pl.ds(h * half_lanes, half_lanes)],
                leg_sem.at[2 * h + p],
            )
            for p in range(2)
        ]
        for h in range(2)
    ]
    tab_copy = pltpu.make_async_copy(tab_hbm, tab0, tab_sem)
    small_copies = [
        pltpu.make_async_copy(src, dst, small_sem.at[n])
        for n, (src, dst) in enumerate(
            ((first_hbm, first_row), (counts_hbm, counts), (weights_hbm, weights), (coeffs_hbm, coeffs))
        )
    ]
    for copy in small_copies + leg_copies[0] + leg_copies[1]:
        copy.start()

    barrier = pltpu.get_barrier_semaphore()
    x_line = [device(z_me, x_me + i, y_me, c_me) for i in range(1, 4)]
    lev_group = [device(z_me, x_me, y_me + i // 2, c_me + i % 2) for i in range(1, LEVS)]
    for to in [device(z_me + i, x_me, y_me, c_me) for i in range(1, 8)] + x_line + lev_group:
        signal(barrier, to)

    for copy in small_copies:
        copy.wait()
    firsts = first_row[...].reshape(1, HALF)
    slots = lax.broadcasted_iota(jnp.int32, (1, HALF), 1)
    entry = lax.broadcasted_iota(jnp.int32, (1, PAIRLEN), 1)
    alternating = (1 - 2 * (entry % 2)).astype(F32)
    masks, signs, spreads, scales = [], [], [], []
    quad = weights[...].reshape(1, HLAT)
    limits = jnp.minimum(WAVES - 1, counts[...].reshape(1, 2 * HLAT) // 2 - 1)
    flip = (
        lax.broadcasted_iota(jnp.int32, (LANES, LANES), 0) + lax.broadcasted_iota(jnp.int32, (LANES, LANES), 1)
        == LANES - 1
    ).astype(BF16)
    tiles = jnp.concatenate(
        [limits[:, (2 * LTILES - 1 - t) * LANES : (2 * LTILES - t) * LANES] for t in range(LTILES)]
        + [jnp.zeros((16 - LTILES, LANES), jnp.int32)],
        axis=0,
    )
    high, low = tiles // 32, tiles % 32
    mirrored = 32.0 * jnp.dot(high.astype(F32).astype(BF16), flip, preferred_element_type=F32) + jnp.dot(
        low.astype(F32).astype(BF16), flip, preferred_element_type=F32
    )
    south = jnp.concatenate([mirrored[t : t + 1, :] for t in range(LTILES)], axis=1)
    sides = (limits[:, :HLAT].astype(F32), south)
    for p in range(2):
        first = jnp.sum(jnp.where(slots == 2 * me + p, firsts, 0), axis=1, keepdims=True)
        border = WAVES - first
        is_odd = first % 2
        one = (entry < border).astype(F32)
        two = ((entry >= border) & (entry <= WAVES)).astype(F32)
        odd = is_odd.astype(F32)
        masks.append((one + odd * (two - one), two + odd * (one - two)))
        signs.append((alternating * (1.0 - 2.0 * odd), alternating))
        even_wave = first + is_odd * (WAVES - 1 - 2 * first)
        waves = [w.astype(F32) for w in (even_wave, WAVES - 1 - even_wave)]
        kept = [[(sides[s] >= w).astype(F32) for w in waves] for s in range(2)]
        scales.append([[kept[s][par] * jnp.where(waves[par] == 0, 1.0, 2.0) for par in range(2)] for s in range(2)])
        rows = []
        for side in range(2):
            for c in range(2):
                values = coeffs[p, c].astype(F32)
                for par in range(2):
                    rows.append(values * (masks[p][par] * signs[p][par] if side else masks[p][par]))
                    kind = p * 8 + side * 4 + c * 2 + par
                    mw[kind : kind + 1, :] = kept[side][par] * quad
        spreads.append(jnp.concatenate(rows, axis=0).astype(BF16))

    def inverse(h, p):
        leg_copies[h][p].wait()
        for lt, count in ((0, 2), (2, 2), (4, 1)):
            at = slice(h * half_lanes + lt * LANES, h * half_lanes + (lt + count) * LANES)
            product = jnp.dot(spreads[p], leg[p, :, at], preferred_element_type=F32)
            for side in range(2):
                for par in range(2):
                    scale = scales[p][side][par][:, at]
                    for c in range(2):
                        kind = side * 4 + c * 2 + par
                        piece = product[kind * KIN : (kind + 1) * KIN] * scale
                        for n in range(count):
                            ys[h * 5 + lt + n, p * 192 + kind * KIN : p * 192 + (kind + 1) * KIN, :] = piece[
                                :, n * LANES : (n + 1) * LANES
                            ]

    lane16 = lane_iota(16)

    def make_and_send(h, core):
        def step(i, carry):
            b = (((y_me + i) & 3) << 1) + core
            fields = [
                [ys[h * 5 + lt, pl.ds(3 * b + f, 16, stride=KIN), :] for lt in range(5)] for f in range(3)
            ]
            for n in range(16):
                tile, shift = divmod(n * RLEN, LANES)
                parts = []
                for f in range(3):
                    part = fields[f][tile]
                    if shift + RLEN > LANES:
                        part = jnp.where(lane16 >= shift, part, fields[f][tile + 1])
                    parts.append(left(part, shift - f * RLEN))
                block = jnp.where(lane16 < RLEN, parts[0], jnp.where(lane16 < 2 * RLEN, parts[1], parts[2]))
                send[h * 16 + n, b] = block.astype(BF16)

            def go(l, carry):
                z, x = (z_me + l) & 7, 2 * h + (((l >> 3) + x_me) & 1)
                a = (z << 2) + x

                @pl.when((b != b_me) | (a != a_me))
                def _():
                    pltpu.make_async_remote_copy(
                        src_ref=send.at[(x << 3) + z, b],
                        dst_ref=recv.at[me],
                        send_sem=send_sem,
                        recv_sem=recv_sem,
                        device_id=(a, b),
                        device_id_type=MESH,
                    ).start()

                return carry

            lax.fori_loop(0, 16, go, 0)
            return carry

        lax.fori_loop(0, 4, step, 0)

    pl.semaphore_wait(barrier, 17)
    for to in x_line:
        signal(round_sem.at[0], to)
    inverse(0, 0)
    pl.semaphore_wait(round_sem.at[0], 3)
    for to in lev_group:
        signal(round_sem.at[1], to)
    inverse(0, 1)
    tab_copy.start()
    pl.semaphore_wait(round_sem.at[1], LEVS - 1)
    make_and_send(0, 0)
    for p in range(2):
        inverse(1, p)
    make_and_send(1, 0)
    make_and_send(0, 1)
    make_and_send(1, 1)
    own = pltpu.make_async_copy(send.at[(x_me << 3) + z_me, b_me], recv.at[me], own_sem)
    own.start()

    tab_copy.wait()
    slot_row = jnp.where(firsts % 2 == 0, firsts, WAVES - 1 - firsts) // 2
    chosen = (lax.broadcasted_iota(jnp.int32, (HALF, HALF), 0) == slot_row).astype(F32)
    pick = jnp.transpose(chosen).astype(BF16)

    def permute(n, carry):
        at = pl.ds(pl.multiple_of(n * 256, 256), 256)
        tab[:, at] = jnp.dot(pick, tab0[:, at], preferred_element_type=F32).astype(BF16)
        return carry

    lax.fori_loop(0, 4 * JPAD // 256, permute, 0)

    own.wait()
    others = pl.ds(0, DEVICES - 1)
    away = ((3, 5), (4, 0), (2, 6), (1, 7))

    def middle():
        pltpu.make_async_copy(recv.at[others], recv.at[others], recv_sem).wait()

        def unpack(n, carry):
            blocks = recv[pl.ds(n * 16, 16)].astype(F32).reshape(256, LANES)
            xs[pl.ds(pl.multiple_of(n * 256, 256), 256), :] = blocks
            return carry

        lax.fori_loop(0, DEVICES // 16, unpack, 0)
        for side in range(2):
            for cp in range(4):
                for q in range(4):
                    block = xs[pl.ds(q * 1024 + side * 4 + cp, LANES, stride=8), :]
                    xt[cp, side * LANES : (side + 1) * LANES, q * LANES : (q + 1) * LANES] = jnp.transpose(
                        block
                    ).astype(BF16)

        for cp in range(4):
            for side in range(2):
                flux[cp, side * LANES + 2 * RLEN : (side + 1) * LANES, :] = jnp.zeros((LANES - 2 * RLEN, JPAD), BF16)
        for at, width in JTILES:
            ce, co, se, so = (
                jnp.dot(xt[cp], tab[:, cp * JPAD + at : cp * JPAD + at + width], preferred_element_type=F32)
                for cp in range(4)
            )
            column = at + lax.broadcasted_iota(jnp.int32, (1, width), 1)
            half = jnp.where((column == 0) | (column == QUARTER), 0.5, 1.0)
            plus, minus, sums, diffs = ce + co, ce - co, se + so, se - so
            grids = (plus + sums, plus - sums, minus - diffs, minus + diffs)
            for side in range(2):
                base = side * LANES
                fl = []
                for g in grids:
                    q = g[base + 2 * RLEN : base + 3 * RLEN] * half
                    fl.append(g[base : base + 2 * RLEN] * jnp.concatenate([q, q], axis=0))
                s12, d12, s34, d34 = fl[0] + fl[1], fl[0] - fl[1], fl[2] + fl[3], fl[3] - fl[2]
                for cp, value in enumerate((s12 + s34, s12 - s34, d12 + d34, d12 - d34)):
                    flux[cp, base : base + 2 * RLEN, at : at + width] = value.astype(BF16)

        for cp in range(4):
            spectra = lax.dot_general(
                tab[:, cp * JPAD : (cp + 1) * JPAD], flux[cp], (((1,), (1,)), ((), ())), preferred_element_type=F32
            )
            for side in range(2):
                xs[pl.ds(side * 4 + cp, HALF, stride=8), :] = spectra[:, side * LANES : (side + 1) * LANES]

    def pack(core, part):
        z = [(z_me + dz) & 7 for dz in away[part]]

        def step(i, carry):
            b = ((((i >> 1) + y_me) & 3) << 1) + ((i + c_me) & 1)
            rows = [
                xs[pl.ds(pl.multiple_of(((((z[n // 4] << 2) + n % 4) << 3) + b) * 16, 16), 16), :] for n in range(8)
            ]
            turned = jnp.transpose(jnp.concatenate(rows, axis=0))
            send_lev[part, b] = turned[: 2 * RLEN].astype(BF16)

            @pl.when(i > 0)
            def _():
                pltpu.make_async_remote_copy(
                    src_ref=send_lev.at[part, b],
                    dst_ref=mid.at[core, part, y_me],
                    send_sem=lev_send_sem,
                    recv_sem=lev_recv_sem.at[core, part],
                    device_id=(a_me, b),
                    device_id_type=MESH,
                ).start()

            return carry

        lax.fori_loop(0, LEVS, step, 0)
        mid[core, part, y_me] = send_lev[part, b_me]

    lane40 = lane_iota(RLEN) // 16
    no_rows = jnp.zeros((8, LANES), F32)

    def relay(core, part):
        for present in (3, 4):

            @pl.when(c_me == (core if present == 3 else 1 - core))
            def _():
                arrived = mid.at[core, part, pl.ds(0, present)]
                pltpu.make_async_copy(arrived, arrived, lev_recv_sem.at[core, part]).wait()

        both = [mid[core, part, y].astype(F32) for y in range(4)]
        arrays = [both[y][comp * RLEN : (comp + 1) * RLEN] for comp in range(2) for y in range(4)]
        for bit in (1, 2, 4):
            low = lane40 & bit == 0
            swapped = list(arrays)
            for n in range(8):
                if not n & bit:
                    one, two = arrays[n], arrays[n + bit]
                    swapped[n] = jnp.where(low, one, pltpu.roll(two, bit * 16, 1))
                    swapped[n + bit] = jnp.where(low, pltpu.roll(one, LANES - bit * 16, 1), two)
            arrays = swapped
        pair = away[part]
        for n in range(8):
            z = (z_me + pair[n // 4]) & 7
            send_lat[core, (z << 2) + n % 4] = jnp.concatenate([arrays[n], no_rows], axis=0).astype(BF16)

        def go(l, carry):
            z, x = (z_me + jnp.where(l < 4, pair[0], pair[1])) & 7, (x_me + l) & 3
            a = (z << 2) + x

            @pl.when(a != a_me)
            def _():
                pltpu.make_async_remote_copy(
                    src_ref=send_lat.at[core, a],
                    dst_ref=last.at[core, a_me],
                    send_sem=lat_send_sem,
                    recv_sem=lat_recv_sem.at[core],
                    device_id=(a, b_me),
                    device_id_type=MESH,
                ).start()

            return carry

        lax.fori_loop(0, 8, go, 0)

    for core in range(2):

        @pl.when(c_me == core)
        def _():
            middle()
            for part in range(4):
                pack(core, part)

        for part in range(4):
            relay(core, part)
        last[core, a_me] = send_lat[core, a_me]

    rest = pl.ds(0, LATS - 1)
    for core in range(2):
        arrived = last.at[core, rest]
        pltpu.make_async_copy(arrived, arrived, lat_recv_sem.at[core]).wait()
        for a in range(LATS):
            at = ((a % 4) * 8 + a // 4) * RLEN
            dt[core, at : at + RLEN, :] = last[core, a].astype(F32)[:RLEN]
    for lt in range(LTILES):
        at = slice(lt * LANES, (lt + 1) * LANES)
        turned = [jnp.transpose(dt[core, at, :]) for core in range(2)]
        for p in range(2):
            weight = mw[p * 8 : p * 8 + 8, at]
            dsp[p, :, at] = jnp.concatenate(
                [
                    turned[b % 2][comp * 64 + b // 2 * 16 + p * 8 : comp * 64 + b // 2 * 16 + p * 8 + 8] * weight
                    for b in range(LEVS)
                    for comp in range(2)
                ],
                axis=0,
            ).astype(BF16)
    for p in range(2):
        product = lax.dot_general(leg[p], dsp[p], (((1,), (1,)), ((), ())), preferred_element_type=F32)
        for n in range(PAIRLEN // LANES):
            at = slice(n * LANES, (n + 1) * LANES)
            rs[n] = jnp.transpose(product[at])
            for c in range(2):
                total = None
                for par in range(2):
                    north = rs[n, pl.ds(c * 2 + par, 16, stride=8), :]
                    south = rs[n, pl.ds(4 + c * 2 + par, 16, stride=8), :]
                    term = masks[p][par][:, at] * (north + signs[p][par][:, at] * south)
                    total = term if total is None else total + term
                out[p, c, :, at] = total.astype(BF16)

    sent = send_lev.at[:, pl.ds(0, LEVS - 1)]
    pltpu.make_async_copy(recv.at[others], recv.at[others], send_sem).wait()
    pltpu.make_async_copy(sent, sent, lev_send_sem).wait()
    pltpu.make_async_copy(last.at[:, rest], last.at[:, rest], lat_send_sem).wait()


def on_device(table, coeffs, legendre, pair_first, row_counts, quad_weights):
    swapped = coeffs.transpose(2, 1, 0, 3)
    vmem = pl.BlockSpec(memory_space=pltpu.VMEM)
    hbm = pl.BlockSpec(memory_space=pltpu.HBM)
    result = pl.pallas_call(
        kernel,
        out_shape=jax.ShapeDtypeStruct((2, 2, 16, PAIRLEN), BF16),
        in_specs=[hbm] * 6,
        out_specs=vmem,
        scratch_shapes=[
            pltpu.VMEM((2, 2, KIN, PAIRLEN), BF16),
            pltpu.VMEM((HALF,), jnp.int32),
            pltpu.VMEM((2 * HLAT,), jnp.int32),
            pltpu.VMEM((HLAT,), F32),
            pltpu.VMEM((2, PAIRLEN, HLAT), BF16),
            pltpu.VMEM((HALF, 4 * JPAD), BF16),
            pltpu.VMEM((HALF, 4 * JPAD), BF16),
            pltpu.VMEM((LTILES, 384, LANES), F32),
            pltpu.VMEM((LATS, LEVS, 16, LANES), BF16),
            pltpu.VMEM((DEVICES, 16, LANES), BF16),
            pltpu.VMEM((DEVICES * 16, LANES), F32),
            pltpu.VMEM((4, 256, HALF), BF16),
            pltpu.VMEM((4, 256, JPAD), BF16),
            pltpu.VMEM((4, LEVS, 2 * RLEN, LANES), BF16),
            pltpu.VMEM((2, 4, 4, 2 * RLEN, LANES), BF16),
            pltpu.VMEM((2, LATS, RLEN + 8, LANES), BF16),
            pltpu.VMEM((2, LATS, RLEN + 8, LANES), BF16),
            pltpu.VMEM((2, HLAT, LANES), F32),
            pltpu.VMEM((2, 128, HLAT), BF16),
            pltpu.VMEM((PAIRLEN // LANES, 128, LANES), F32),
            pltpu.VMEM((16, HLAT), F32),
            pltpu.SemaphoreType.DMA((4,)),
            pltpu.SemaphoreType.DMA,
            pltpu.SemaphoreType.DMA,
            pltpu.SemaphoreType.DMA,
            pltpu.SemaphoreType.DMA,
            pltpu.SemaphoreType.DMA,
            pltpu.SemaphoreType.DMA((2, 4)),
            pltpu.SemaphoreType.DMA,
            pltpu.SemaphoreType.DMA((2,)),
            pltpu.SemaphoreType.REGULAR((2,)),
            pltpu.SemaphoreType.DMA((4,)),
        ],
        compiler_params=pltpu.CompilerParams(
            collective_id=0, has_side_effects=True, vmem_limit_bytes=62 * 2**20
        ),
        name="transforms",
    )(swapped, legendre, table, pair_first, row_counts, quad_weights)
    return result.transpose(2, 1, 0, 3)


def solution(mesh):
    placed = (P(None, None, ("lat", "lev"), None), P(("lat", "lev"), None, None), P(), P(), P())
    table = table_constant()
    return jax.shard_map(
        functools.partial(on_device, table),
        mesh=mesh,
        in_specs=placed,
        out_specs=P(None, None, ("lat", "lev"), None),
        check_vma=False,
    )
```

time: 80 us -> 71.6 us (0.89)
  Pallas kernels: 75.7 us -> 68.2 us
    pallas_call x1, Pallas kernels: 75.7 us -> 68.2 us  [on_device(): pl.pallas_call(kernel, out_shape=jax.ShapeDtypeStruct((2, 2, 16, PAIRLEN)...]
    transpose x1, local copies, waits for them, and re-layouts: 0.78 us -> 1.69 us  [on_device(): return result.transpose(2, 1, 0, 3)]
    unnamed x3 -> x1, local copies, waits for them, and re-layouts: 1.64 us -> 1.63 us
where the time goes in v2:
time: 71.6 us; the launch traced here: 71.5 us
  Pallas kernels  68.2 us (95%)
  local copies, waits for them, and re-layouts  3.32 us (5%)
    pallas_call x1, Pallas kernels, on_device(): pl.pallas_call(kernel, out_shape=jax.ShapeDtypeStruct((2, 2, 16, PAIRLEN)...  68.2 us
    transpose x1, local copies, waits for them, and re-layouts, on_device(): return result.transpose(2, 1, 0, 3)  1.69 us
    unnamed x1, local copies, waits for them, and re-layouts  1.63 us

profile of v2, /device:TPU:1, one launch (start us, length us, event | category | flops | bytes accessed | tf_op | source)
XLA Modules:
  0.0 71.5 jit_solution(9187302439052260087)
XLA Ops:
  0.0 1.6 %copy.10 = bf16[24,2,2,1152]{3,0,1,2:T(8,128)(2,1)} copy(bf16[24,2,2,1152]{3,2,1,0:T(2,128)(2,1)} %param.6) | data formatting | bytes 442368 | tf_op args[0]
  1.6 68.2 %transforms.1 = bf16[2,2,16,1152]{3,2,1,0:T(8,128)(2,1)} custom-call(bf16[2,2,24,1152]{3,2,1,0:T(8,128)(2,1)} %bitcast.4, bf16[2,1152,1280]{2,1,0:T(8,128)(2,1)} %leg_hbm.1, bf16[512,5632]{1,0:T(8,128)(2,1)} %constant.2.clone.tab_hbm, s32[512]{0:T(512)} %first_hbm.1, s32[2560]{0:T(1024)} %counts_hbm.1, f32[1280]{0:T(1024)} %weights_hbm.1), custom_call_target="tpu_custom_call" | custom-call | tf_op jit(solution)/shard_map/transforms/pallas_call | solution.py:419
  69.8 1.7 %copy.8 = bf16[16,2,2,1152]{3,2,1,0:T(2,128)(2,1)} copy(bf16[16,2,2,1152]{3,0,1,2:T(8,128)(2,1)} %bitcast.5) | data formatting | bytes 294912 | tf_op jit(solution)/shard_map/transpose | solution.py:463

commit v3 on v2

--- a/solution.py
+++ b/solution.py
@@ -66,7 +66,7 @@
 
 def kernel(
     coeffs_hbm, leg_hbm, tab_hbm, first_hbm, counts_hbm, weights_hbm, out,
-    coeffs, first_row, counts, weights, leg, tab0, tab, ys, send, recv, xs, xt, flux, send_lev, mid, send_lat, last, dt, dsp, rs, mw,
+    coeffs, lines, res, first_row, counts, weights, leg, tab0, tab, ys, send, recv, xs, xt, flux, send_lev, mid, send_lat, last, dt, dsp, rs, mw,
     leg_sem, tab_sem, own_sem, send_sem, recv_sem, lev_send_sem, lev_recv_sem, lat_send_sem, lat_recv_sem,
     round_sem, small_sem,
 ):
@@ -109,6 +109,9 @@
     entry = lax.broadcasted_iota(jnp.int32, (1, PAIRLEN), 1)
     alternating = (1 - 2 * (entry % 2)).astype(F32)
     masks, signs, spreads, scales = [], [], [], []
+    unrolled = coeffs[...].astype(F32).reshape(4 * KIN, PAIRLEN)
+    for n in range(PAIRLEN // LANES):
+        lines[n] = unrolled[:, n * LANES : (n + 1) * LANES]
     quad = weights[...].reshape(1, HLAT)
     limits = jnp.minimum(WAVES - 1, counts[...].reshape(1, 2 * HLAT) // 2 - 1)
     flip = (
@@ -142,7 +145,9 @@
         rows = []
         for side in range(2):
             for c in range(2):
-                values = coeffs[p, c].astype(F32)
+                values = jnp.concatenate(
+                    [lines[n, pl.ds(2 * c + p, KIN, stride=4), :] for n in range(PAIRLEN // LANES)], axis=1
+                )
                 for par in range(2):
                     rows.append(values * (masks[p][par] * signs[p][par] if side else masks[p][par]))
                     kind = p * 8 + side * 4 + c * 2 + par
@@ -167,7 +172,7 @@
 
     lane16 = lane_iota(16)
 
-    def make_and_send(h, core):
+    def make_and_send(h, core, first=0, last=4):
         def step(i, carry):
             b = (((y_me + i) & 3) << 1) + core
             fields = [
@@ -204,7 +209,7 @@
             lax.fori_loop(0, 16, go, 0)
             return carry
 
-        lax.fori_loop(0, 4, step, 0)
+        lax.fori_loop(first, last, step, 0)
 
     pl.semaphore_wait(barrier, 17)
     for to in x_line:
@@ -220,11 +225,6 @@
     for p in range(2):
         inverse(1, p)
     make_and_send(1, 0)
-    make_and_send(0, 1)
-    make_and_send(1, 1)
-    own = pltpu.make_async_copy(send.at[(x_me << 3) + z_me, b_me], recv.at[me], own_sem)
-    own.start()
-
     tab_copy.wait()
     slot_row = jnp.where(firsts % 2 == 0, firsts, WAVES - 1 - firsts) // 2
     chosen = (lax.broadcasted_iota(jnp.int32, (HALF, HALF), 0) == slot_row).astype(F32)
@@ -237,145 +237,143 @@
 
     lax.fori_loop(0, 4 * JPAD // 256, permute, 0)
 
+    make_and_send(0, 1)
+
+    make_and_send(1, 1)
+
+    own = pltpu.make_async_copy(send.at[(x_me << 3) + z_me, b_me], recv.at[me], own_sem)
+    own.start()
+
     own.wait()
     others = pl.ds(0, DEVICES - 1)
     away = ((3, 5), (4, 0), (2, 6), (1, 7))
 
-    def middle():
-        pltpu.make_async_copy(recv.at[others], recv.at[others], recv_sem).wait()
-
-        def unpack(n, carry):
-            blocks = recv[pl.ds(n * 16, 16)].astype(F32).reshape(256, LANES)
-            xs[pl.ds(pl.multiple_of(n * 256, 256), 256), :] = blocks
-            return carry
-
-        lax.fori_loop(0, DEVICES // 16, unpack, 0)
+    pltpu.make_async_copy(recv.at[others], recv.at[others], recv_sem).wait()
+
+    def unpack(n, carry):
+        blocks = recv[pl.ds(n * 16, 16)].astype(F32).reshape(256, LANES)
+        xs[pl.ds(pl.multiple_of(n * 256, 256), 256), :] = blocks
+        return carry
+
+    lax.fori_loop(0, DEVICES // 16, unpack, 0)
+    for side in range(2):
+        for cp in range(4):
+            for q in range(4):
+                block = xs[pl.ds(q * 1024 + side * 4 + cp, LANES, stride=8), :]
+                xt[cp, side * LANES : (side + 1) * LANES, q * LANES : (q + 1) * LANES] = jnp.transpose(
+                    block
+                ).astype(BF16)
+
+    for cp in range(4):
         for side in range(2):
-            for cp in range(4):
-                for q in range(4):
-                    block = xs[pl.ds(q * 1024 + side * 4 + cp, LANES, stride=8), :]
-                    xt[cp, side * LANES : (side + 1) * LANES, q * LANES : (q + 1) * LANES] = jnp.transpose(
-                        block
-                    ).astype(BF16)
-
-        for cp in range(4):
-            for side in range(2):
-                flux[cp, side * LANES + 2 * RLEN : (side + 1) * LANES, :] = jnp.zeros((LANES - 2 * RLEN, JPAD), BF16)
-        for at, width in JTILES:
-            ce, co, se, so = (
-                jnp.dot(xt[cp], tab[:, cp * JPAD + at : cp * JPAD + at + width], preferred_element_type=F32)
-                for cp in range(4)
-            )
-            column = at + lax.broadcasted_iota(jnp.int32, (1, width), 1)
-            half = jnp.where((column == 0) | (column == QUARTER), 0.5, 1.0)
-            plus, minus, sums, diffs = ce + co, ce - co, se + so, se - so
-            grids = (plus + sums, plus - sums, minus - diffs, minus + diffs)
-            for side in range(2):
-                base = side * LANES
-                fl = []
-                for g in grids:
-                    q = g[base + 2 * RLEN : base + 3 * RLEN] * half
-                    fl.append(g[base : base + 2 * RLEN] * jnp.concatenate([q, q], axis=0))
-                s12, d12, s34, d34 = fl[0] + fl[1], fl[0] - fl[1], fl[2] + fl[3], fl[3] - fl[2]
-                for cp, value in enumerate((s12 + s34, s12 - s34, d12 + d34, d12 - d34)):
-                    flux[cp, base : base + 2 * RLEN, at : at + width] = value.astype(BF16)
-
-        for cp in range(4):
-            spectra = lax.dot_general(
-                tab[:, cp * JPAD : (cp + 1) * JPAD], flux[cp], (((1,), (1,)), ((), ())), preferred_element_type=F32
-            )
-            for side in range(2):
-                xs[pl.ds(side * 4 + cp, HALF, stride=8), :] = spectra[:, side * LANES : (side + 1) * LANES]
-
-    def pack(core, part):
+            flux[cp, side * LANES + 2 * RLEN : (side + 1) * LANES, :] = jnp.zeros((LANES - 2 * RLEN, JPAD), BF16)
+    for at, width in JTILES:
+        ce, co, se, so = (
+            jnp.dot(xt[cp], tab[:, cp * JPAD + at : cp * JPAD + at + width], preferred_element_type=F32)
+            for cp in range(4)
+        )
+        column = at + lax.broadcasted_iota(jnp.int32, (1, width), 1)
+        half = jnp.where((column == 0) | (column == QUARTER), 0.5, 1.0)
+        plus, minus, sums, diffs = ce + co, ce - co, se + so, se - so
+        grids = (plus + sums, plus - sums, minus - diffs, minus + diffs)
+        for side in range(2):
+            base = side * LANES
+            fl = []
+            for g in grids:
+                q = g[base + 2 * RLEN : base + 3 * RLEN] * half
+                fl.append(g[base : base + 2 * RLEN] * jnp.concatenate([q, q], axis=0))
+            s12, d12, s34, d34 = fl[0] + fl[1], fl[0] - fl[1], fl[2] + fl[3], fl[3] - fl[2]
+            for cp, value in enumerate((s12 + s34, s12 - s34, d12 + d34, d12 - d34)):
+                flux[cp, base : base + 2 * RLEN, at : at + width] = value.astype(BF16)
+
+
+    for cp in range(4):
+        spectra = lax.dot_general(
+            tab[:, cp * JPAD : (cp + 1) * JPAD], flux[cp], (((1,), (1,)), ((), ())), preferred_element_type=F32
+        )
+        for side in range(2):
+            xs[pl.ds(side * 4 + cp, HALF, stride=8), :] = spectra[:, side * LANES : (side + 1) * LANES]
+
+    def pack(part):
         z = [(z_me + dz) & 7 for dz in away[part]]
 
-        def step(i, carry):
-            b = ((((i >> 1) + y_me) & 3) << 1) + ((i + c_me) & 1)
+        for i in range(LEVS):
+            b = (((y_me + i // 2) & 3) << 1) + i % 2
             rows = [
                 xs[pl.ds(pl.multiple_of(((((z[n // 4] << 2) + n % 4) << 3) + b) * 16, 16), 16), :] for n in range(8)
             ]
             turned = jnp.transpose(jnp.concatenate(rows, axis=0))
             send_lev[part, b] = turned[: 2 * RLEN].astype(BF16)
 
-            @pl.when(i > 0)
+        def go(i, carry):
+            y, c = (y_me + (i >> 1)) & 3, i & 1
+            pltpu.make_async_remote_copy(
+                src_ref=send_lev.at[part, (y << 1) + c],
+                dst_ref=mid.at[part, c, y_me],
+                send_sem=lev_send_sem,
+                recv_sem=lev_recv_sem.at[part],
+                device_id=(a_me, (y << 1) + c_me),
+                device_id_type=MESH,
+            ).start()
+            return carry
+
+        lax.fori_loop(2, LEVS, go, 0)
+        for c in range(2):
+            mid[part, c, y_me] = send_lev[part, (y_me << 1) + c]
+
+    for part in range(4):
+        pack(part)
+
+
+    lane40 = lane_iota(RLEN) // 16
+    no_rows = jnp.zeros((8, LANES), F32)
+    for part, pair in enumerate(away):
+        arrived = mid.at[part, :, pl.ds(0, 3)]
+        pltpu.make_async_copy(arrived, arrived, lev_recv_sem.at[part]).wait()
+        for c in range(2):
+            both = [mid[part, c, y].astype(F32) for y in range(4)]
+            arrays = [both[y][comp * RLEN : (comp + 1) * RLEN] for comp in range(2) for y in range(4)]
+            for bit in (1, 2, 4):
+                low = lane40 & bit == 0
+                swapped = list(arrays)
+                for n in range(8):
+                    if not n & bit:
+                        one, two = arrays[n], arrays[n + bit]
+                        swapped[n] = jnp.where(low, one, pltpu.roll(two, bit * 16, 1))
+                        swapped[n + bit] = jnp.where(low, pltpu.roll(one, LANES - bit * 16, 1), two)
+                arrays = swapped
+            for n in range(8):
+                z = (z_me + pair[n // 4]) & 7
+                send_lat[c * LATS + (z << 2) + n % 4] = jnp.concatenate([arrays[n], no_rows], axis=0).astype(BF16)
+
+        def relay(l, carry):
+            z, x, c = (z_me + jnp.where(l & 4 == 0, pair[0], pair[1])) & 7, (x_me + l) & 3, (c_me + (l >> 3)) & 1
+            a = (z << 2) + x
+
+            @pl.when((a != a_me) | (c != c_me))
             def _():
                 pltpu.make_async_remote_copy(
-                    src_ref=send_lev.at[part, b],
-                    dst_ref=mid.at[core, part, y_me],
-                    send_sem=lev_send_sem,
-                    recv_sem=lev_recv_sem.at[core, part],
-                    device_id=(a_me, b),
+                    src_ref=send_lat.at[(c << 5) + a],
+                    dst_ref=last.at[c_me, a_me],
+                    send_sem=lat_send_sem,
+                    recv_sem=lat_recv_sem.at[c_me],
+                    device_id=(a, (y_me << 1) + c),
                     device_id_type=MESH,
                 ).start()
 
             return carry
 
-        lax.fori_loop(0, LEVS, step, 0)
-        mid[core, part, y_me] = send_lev[part, b_me]
-
-    lane40 = lane_iota(RLEN) // 16
-    no_rows = jnp.zeros((8, LANES), F32)
-
-    def relay(core, part):
-        for present in (3, 4):
-
-            @pl.when(c_me == (core if present == 3 else 1 - core))
+        lax.fori_loop(0, 16, relay, 0)
+    last[c_me, a_me] = send_lat[(c_me << 5) + a_me]
+
+    for core in range(2):
+        for count in (LATS - 1, LATS):
+
+            @pl.when(c_me == (core if count < LATS else 1 - core))
             def _():
-                arrived = mid.at[core, part, pl.ds(0, present)]
-                pltpu.make_async_copy(arrived, arrived, lev_recv_sem.at[core, part]).wait()
-
-        both = [mid[core, part, y].astype(F32) for y in range(4)]
-        arrays = [both[y][comp * RLEN : (comp + 1) * RLEN] for comp in range(2) for y in range(4)]
-        for bit in (1, 2, 4):
-            low = lane40 & bit == 0
-            swapped = list(arrays)
-            for n in range(8):
-                if not n & bit:
-                    one, two = arrays[n], arrays[n + bit]
-                    swapped[n] = jnp.where(low, one, pltpu.roll(two, bit * 16, 1))
-                    swapped[n + bit] = jnp.where(low, pltpu.roll(one, LANES - bit * 16, 1), two)
-            arrays = swapped
-        pair = away[part]
-        for n in range(8):
-            z = (z_me + pair[n // 4]) & 7
-            send_lat[core, (z << 2) + n % 4] = jnp.concatenate([arrays[n], no_rows], axis=0).astype(BF16)
-
-        def go(l, carry):
-            z, x = (z_me + jnp.where(l < 4, pair[0], pair[1])) & 7, (x_me + l) & 3
-            a = (z << 2) + x
-
-            @pl.when(a != a_me)
-            def _():
-                pltpu.make_async_remote_copy(
-                    src_ref=send_lat.at[core, a],
-                    dst_ref=last.at[core, a_me],
-                    send_sem=lat_send_sem,
-                    recv_sem=lat_recv_sem.at[core],
-                    device_id=(a, b_me),
-                    device_id_type=MESH,
-                ).start()
-
-            return carry
-
-        lax.fori_loop(0, 8, go, 0)
-
-    for core in range(2):
-
-        @pl.when(c_me == core)
-        def _():
-            middle()
-            for part in range(4):
-                pack(core, part)
-
-        for part in range(4):
-            relay(core, part)
-        last[core, a_me] = send_lat[core, a_me]
-
-    rest = pl.ds(0, LATS - 1)
-    for core in range(2):
-        arrived = last.at[core, rest]
-        pltpu.make_async_copy(arrived, arrived, lat_recv_sem.at[core]).wait()
+                arrived = last.at[core, pl.ds(0, count)]
+                pltpu.make_async_copy(arrived, arrived, lat_recv_sem.at[core]).wait()
+
         for a in range(LATS):
             at = ((a % 4) * 8 + a // 4) * RLEN
             dt[core, at : at + RLEN, :] = last[core, a].astype(F32)[:RLEN]
@@ -404,25 +402,29 @@
                     south = rs[n, pl.ds(4 + c * 2 + par, 16, stride=8), :]
                     term = masks[p][par][:, at] * (north + signs[p][par][:, at] * south)
                     total = term if total is None else total + term
-                out[p, c, :, at] = total.astype(BF16)
-
-    sent = send_lev.at[:, pl.ds(0, LEVS - 1)]
+                res[n, pl.ds(2 * c + p, 16, stride=4), :] = total
+
+    for n in range(PAIRLEN // LANES):
+        out[:, :, :, n * LANES : (n + 1) * LANES] = res[n].astype(BF16).reshape(16, 2, 2, LANES)
     pltpu.make_async_copy(recv.at[others], recv.at[others], send_sem).wait()
+    sent = send_lev.at[:, pl.ds(0, 6)]
     pltpu.make_async_copy(sent, sent, lev_send_sem).wait()
-    pltpu.make_async_copy(last.at[:, rest], last.at[:, rest], lat_send_sem).wait()
+    sent = send_lat.at[pl.ds(0, 2 * LATS - 1)]
+    pltpu.make_async_copy(sent, sent, lat_send_sem).wait()
 
 
 def on_device(table, coeffs, legendre, pair_first, row_counts, quad_weights):
-    swapped = coeffs.transpose(2, 1, 0, 3)
     vmem = pl.BlockSpec(memory_space=pltpu.VMEM)
     hbm = pl.BlockSpec(memory_space=pltpu.HBM)
     result = pl.pallas_call(
         kernel,
-        out_shape=jax.ShapeDtypeStruct((2, 2, 16, PAIRLEN), BF16),
+        out_shape=jax.ShapeDtypeStruct((16, 2, 2, PAIRLEN), BF16),
         in_specs=[hbm] * 6,
         out_specs=vmem,
         scratch_shapes=[
-            pltpu.VMEM((2, 2, KIN, PAIRLEN), BF16),
+            pltpu.VMEM((KIN, 2, 2, PAIRLEN), BF16),
+            pltpu.VMEM((PAIRLEN // LANES, 4 * KIN, LANES), F32),
+            pltpu.VMEM((PAIRLEN // LANES, 64, LANES), F32),
             pltpu.VMEM((HALF,), jnp.int32),
             pltpu.VMEM((2 * HLAT,), jnp.int32),
             pltpu.VMEM((HLAT,), F32),
@@ -436,8 +438,8 @@
             pltpu.VMEM((4, 256, HALF), BF16),
             pltpu.VMEM((4, 256, JPAD), BF16),
             pltpu.VMEM((4, LEVS, 2 * RLEN, LANES), BF16),
-            pltpu.VMEM((2, 4, 4, 2 * RLEN, LANES), BF16),
-            pltpu.VMEM((2, LATS, RLEN + 8, LANES), BF16),
+            pltpu.VMEM((4, 2, 4, 2 * RLEN, LANES), BF16),
+            pltpu.VMEM((2 * LATS, RLEN + 8, LANES), BF16),
             pltpu.VMEM((2, LATS, RLEN + 8, LANES), BF16),
             pltpu.VMEM((2, HLAT, LANES), F32),
             pltpu.VMEM((2, 128, HLAT), BF16),
@@ -449,7 +451,7 @@
             pltpu.SemaphoreType.DMA,
             pltpu.SemaphoreType.DMA,
             pltpu.SemaphoreType.DMA,
-            pltpu.SemaphoreType.DMA((2, 4)),
+            pltpu.SemaphoreType.DMA((4,)),
             pltpu.SemaphoreType.DMA,
             pltpu.SemaphoreType.DMA((2,)),
             pltpu.SemaphoreType.REGULAR((2,)),
@@ -459,8 +461,8 @@
             collective_id=0, has_side_effects=True, vmem_limit_bytes=62 * 2**20
         ),
         name="transforms",
-    )(swapped, legendre, table, pair_first, row_counts, quad_weights)
-    return result.transpose(2, 1, 0, 3)
+    )(coeffs, legendre, table, pair_first, row_counts, quad_weights)
+    return result
 
 
 def solution(mesh):

time: 71.6 us -> 67.3 us (0.940)
  Pallas kernels: 68.2 us -> 65.5 us
  local copies, waits for them, and re-layouts: 3.32 us -> 1.67 us
    pallas_call x1, Pallas kernels: 68.2 us -> 65.5 us  [on_device(): pl.pallas_call(kernel, out_shape=jax.ShapeDtypeStruct((16, 2, 2, PAIRLEN)...]
    transpose x1 -> x0, local copies, waits for them, and re-layouts: 1.69 us -> none  [on_device(): return result.transpose(2, 1, 0, 3)]
where the time goes in v3:
time: 67.3 us; the launch traced here: 67.2 us
  Pallas kernels  65.5 us (97%)
  local copies, waits for them, and re-layouts  1.67 us (2%)
    pallas_call x1, Pallas kernels, on_device(): pl.pallas_call(kernel, out_shape=jax.ShapeDtypeStruct((16, 2, 2, PAIRLEN)...  65.5 us
    unnamed x1, local copies, waits for them, and re-layouts  1.67 us

profile of v3, /device:TPU:1, one launch (start us, length us, event | category | flops | bytes accessed | tf_op | source)
XLA Modules:
  0.0 67.2 jit_solution(9668073152469454077)
XLA Ops:
  0.0 65.5 %transforms.1 = bf16[16,2,2,1152]{3,2,1,0:T(2,128)(2,1)} custom-call(bf16[24,2,2,1152]{3,2,1,0:T(2,128)(2,1)} %coeffs_hbm.1, bf16[2,1152,1280]{2,1,0:T(8,128)(2,1)} %leg_hbm.1, bf16[512,5632]{1,0:T(8,128)(2,1)} %constant.2.clone.tab_hbm, s32[512]{0:T(512)} %first_hbm.1, s32[2560]{0:T(1024)} %counts_hbm.1, f32[1280]{0:T(1024)} %weights_hbm.1), custom_call_target="tpu_custom_call" | custom-call | tf_op jit(solution)/shard_map/transforms/pallas_call | solution.py:419
  65.6 1.7 %copy.8 = bf16[16,2,2,1152]{3,2,1,0:T(2,128)(2,1)} copy(bf16[16,2,2,1152]{3,2,1,0:T(2,128)(2,1)} %transforms.1) | data formatting | bytes 294912

commit v4 on v3

--- a/solution.py
+++ b/solution.py
@@ -102,6 +102,9 @@
     for to in [device(z_me + i, x_me, y_me, c_me) for i in range(1, 8)] + x_line + lev_group:
         signal(barrier, to)
 
+    pl.semaphore_wait(barrier, 17)
+    for to in x_line:
+        signal(round_sem.at[0], to)
     for copy in small_copies:
         copy.wait()
     firsts = first_row[...].reshape(1, HALF)
@@ -211,13 +214,10 @@
 
         lax.fori_loop(first, last, step, 0)
 
-    pl.semaphore_wait(barrier, 17)
-    for to in x_line:
-        signal(round_sem.at[0], to)
-    inverse(0, 0)
     pl.semaphore_wait(round_sem.at[0], 3)
     for to in lev_group:
         signal(round_sem.at[1], to)
+    inverse(0, 0)
     inverse(0, 1)
     tab_copy.start()
     pl.semaphore_wait(round_sem.at[1], LEVS - 1)
@@ -225,6 +225,13 @@
     for p in range(2):
         inverse(1, p)
     make_and_send(1, 0)
+    make_and_send(0, 1)
+
+    make_and_send(1, 1)
+
+    own = pltpu.make_async_copy(send.at[(x_me << 3) + z_me, b_me], recv.at[me], own_sem)
+    own.start()
+
     tab_copy.wait()
     slot_row = jnp.where(firsts % 2 == 0, firsts, WAVES - 1 - firsts) // 2
     chosen = (lax.broadcasted_iota(jnp.int32, (HALF, HALF), 0) == slot_row).astype(F32)
@@ -237,13 +244,9 @@
 
     lax.fori_loop(0, 4 * JPAD // 256, permute, 0)
 
-    make_and_send(0, 1)
-
-    make_and_send(1, 1)
-
-    own = pltpu.make_async_copy(send.at[(x_me << 3) + z_me, b_me], recv.at[me], own_sem)
-    own.start()
-
+    for cp in range(4):
+        for side in range(2):
+            flux[cp, side * LANES + 2 * RLEN : (side + 1) * LANES, :] = jnp.zeros((LANES - 2 * RLEN, JPAD), BF16)
     own.wait()
     others = pl.ds(0, DEVICES - 1)
     away = ((3, 5), (4, 0), (2, 6), (1, 7))
@@ -255,7 +258,7 @@
         xs[pl.ds(pl.multiple_of(n * 256, 256), 256), :] = blocks
         return carry
 
-    lax.fori_loop(0, DEVICES // 16, unpack, 0)
+    lax.fori_loop(0, DEVICES // 16, unpack, 0, unroll=4)
     for side in range(2):
         for cp in range(4):
             for q in range(4):
@@ -264,9 +267,6 @@
                     block
                 ).astype(BF16)
 
-    for cp in range(4):
-        for side in range(2):
-            flux[cp, side * LANES + 2 * RLEN : (side + 1) * LANES, :] = jnp.zeros((LANES - 2 * RLEN, JPAD), BF16)
     for at, width in JTILES:
         ce, co, se, so = (
             jnp.dot(xt[cp], tab[:, cp * JPAD + at : cp * JPAD + at + width], preferred_element_type=F32)
@@ -377,19 +377,16 @@
         for a in range(LATS):
             at = ((a % 4) * 8 + a // 4) * RLEN
             dt[core, at : at + RLEN, :] = last[core, a].astype(F32)[:RLEN]
-    for lt in range(LTILES):
-        at = slice(lt * LANES, (lt + 1) * LANES)
-        turned = [jnp.transpose(dt[core, at, :]) for core in range(2)]
-        for p in range(2):
-            weight = mw[p * 8 : p * 8 + 8, at]
-            dsp[p, :, at] = jnp.concatenate(
-                [
-                    turned[b % 2][comp * 64 + b // 2 * 16 + p * 8 : comp * 64 + b // 2 * 16 + p * 8 + 8] * weight
-                    for b in range(LEVS)
-                    for comp in range(2)
-                ],
-                axis=0,
-            ).astype(BF16)
+        for lt in range(LTILES):
+            at = slice(lt * LANES, (lt + 1) * LANES)
+            turned = jnp.transpose(dt[core, at, :])
+            for p in range(2):
+                weight = mw[p * 8 : p * 8 + 8, at]
+                for b in range(core, LEVS, 2):
+                    start = b // 2 * 16 + p * 8
+                    both = [turned[comp * 64 + start : comp * 64 + start + 8] * weight for comp in range(2)]
+                    dsp[p, b * 16 : b * 16 + 16, at] = jnp.concatenate(both, axis=0).astype(BF16)
+
     for p in range(2):
         product = lax.dot_general(leg[p], dsp[p], (((1,), (1,)), ((), ())), preferred_element_type=F32)
         for n in range(PAIRLEN // LANES):

time: 67.3 us -> 67 us (level)
  no operation moved by 1% of the time
where the time goes in v4:
time: 67 us; the launch traced here: 66.9 us
  Pallas kernels  65.2 us (97%)
  local copies, waits for them, and re-layouts  1.67 us (2%)
    pallas_call x1, Pallas kernels, on_device(): pl.pallas_call(kernel, out_shape=jax.ShapeDtypeStruct((16, 2, 2, PAIRLEN)...  65.2 us
    unnamed x1, local copies, waits for them, and re-layouts  1.67 us

profile of v4, /device:TPU:1, one launch (start us, length us, event | category | flops | bytes accessed | tf_op | source)
XLA Modules:
  0.0 66.9 jit_solution(6701784938788222170)
XLA Ops:
  0.0 65.2 %transforms.1 = bf16[16,2,2,1152]{3,2,1,0:T(2,128)(2,1)} custom-call(bf16[24,2,2,1152]{3,2,1,0:T(2,128)(2,1)} %coeffs_hbm.1, bf16[2,1152,1280]{2,1,0:T(8,128)(2,1)} %leg_hbm.1, bf16[512,5632]{1,0:T(8,128)(2,1)} %constant.2.clone.tab_hbm, s32[512]{0:T(512)} %first_hbm.1, s32[2560]{0:T(1024)} %counts_hbm.1, f32[1280]{0:T(1024)} %weights_hbm.1), custom_call_target="tpu_custom_call" | custom-call | tf_op jit(solution)/shard_map/transforms/pallas_call | solution.py:416
  65.2 1.7 %copy.8 = bf16[16,2,2,1152]{3,2,1,0:T(2,128)(2,1)} copy(bf16[16,2,2,1152]{3,2,1,0:T(2,128)(2,1)} %transforms.1) | data formatting | bytes 294912
